TPU v7x, 128 devices: a whole 4x4x4 slice. The times are simulated.
128 devices in a mesh: graph: 16 (over x, z), leaf: 8 (over y, core).
Axes of the slice: x: 4, y: 4, z: 4, core: 2. Of those that a mesh axis runs over, the one named last changes fastest.
Arguments:
- features: bfloat16 [32768, 384], P(('graph', 'leaf')), may hold values from -6 to 6
- send_rows: int32 [128, 128, 32], P(('graph', 'leaf')), may hold values from 0 to 255
- neighbour_slot: int32 [32768, 16], P(('graph', 'leaf')), may hold values from 0 to 4095, as said below
- degree: int32 [32768], P(('graph', 'leaf')), may hold values from 1 to 16
- self_weight: bfloat16 [384, 512], replicated, may hold values from -0.3125 to 0.3125
- neigh_weight: bfloat16 [384, 512], replicated, may hold values from -0.3125 to 0.3125
- hidden_bias: float32 [512], replicated, may hold values from -3 to 3
- out_weight: bfloat16 [512, 64], replicated, may hold values from -0.25 to 0.25
- out_bias: float32 [64], replicated, may hold values from -3 to 3
- out_gain: float32 [64], replicated, may hold values from 0.25 to 1.75
- split_feature: int32 [512, 63], P('leaf'), may hold values from 0 to 447
- threshold: float32 [512, 63], P('leaf'), may hold values from -1 to 1
- leaf_value: float32 [512, 64], P('leaf'), may hold values from -0.6 to 0.6
Outputs:
- embedding: bfloat16 [32768, 64], P(('graph', 'leaf'))
- fraud_score: float32 [32768], P(('graph', 'leaf'))
Inputs may be any that keep to these rules, and one draw needn't show every extreme that they name: `neighbour_slot`: entry [i, j] is a slot s * 32 + k of the buffer that card i's device receives. The slots that one device's cards name from one source s are among the first c of that source, c from 1 to 32 depending on the pair. Only the first degree[i] entries of row i of neighbour_slot count.
All inputs are finite; a program needn't handle non-finite values.
Results may differ from a plain program's by a relative error of at most 0.0047.
Values may be sent and summed in bfloat16 or wider, within the bound.
A program may use at most 64 MiB of HBM per device.

v0:
```python
import jax
import jax.numpy as jnp
from jax import lax
from jax.sharding import PartitionSpec as P

SHARPNESS = 2.0
NORM_EPS = 1e-05


def tree_sums(card_rows, split_ids, cut_points, leaf_scores):
    row_count, feat_width = card_rows.shape
    tree_count, leaf_total = leaf_scores.shape
    depth_count = leaf_total.bit_length() - 1
    block_trees = tree_count
    while block_trees > 1 and (row_count * block_trees > 16384 or tree_count % block_trees != 0):
        block_trees = block_trees // 2
    turn_count = tree_count // block_trees
    node_ids = jnp.concatenate([split_ids, jnp.zeros((tree_count, 1), jnp.int32)], axis=1)
    node_cuts = jnp.concatenate([cut_points, jnp.zeros((tree_count, 1), jnp.float32)], axis=1)
    columns = lax.broadcasted_iota(jnp.int32, (feat_width, 1), 0)

    def one_block(running, blocked):
        block_ids, block_cuts, block_scores = blocked
        selector = (columns == block_ids[None, :]).astype(jnp.bfloat16)
        chosen = jnp.dot(card_rows, selector, preferred_element_type=jnp.float32)
        margin = ((chosen - block_cuts[None, :]) * SHARPNESS).reshape(
            row_count, block_trees, leaf_total
        )
        log_reach = jnp.zeros((row_count, block_trees, 1), jnp.float32)
        for height in range(depth_count):
            first_node = 2**height - 1
            level_margin = margin[:, :, first_node : first_node + 2**height]
            go_left = log_reach + jax.nn.log_sigmoid(-level_margin)
            go_right = log_reach + jax.nn.log_sigmoid(level_margin)
            log_reach = jnp.stack([go_left, go_right], axis=-1).reshape(
                row_count, block_trees, 2 ** (height + 1)
            )
        added = jnp.sum(jnp.exp(log_reach) * block_scores[None], axis=(1, 2))
        return (running + added, None)

    blocked_inputs = (
        node_ids.reshape(turn_count, block_trees * leaf_total),
        node_cuts.reshape(turn_count, block_trees * leaf_total),
        leaf_scores.reshape(turn_count, block_trees, leaf_total),
    )
    return lax.scan(one_block, jnp.zeros((row_count,), jnp.float32), blocked_inputs)[0]


def on_device(
    features,
    send_rows,
    neighbour_slot,
    degree,
    self_weight,
    neigh_weight,
    hidden_bias,
    out_weight,
    out_bias,
    out_gain,
    split_feature,
    threshold,
    leaf_value,
):
    row_count, feat_in = features.shape
    outgoing = jnp.take(features, send_rows[0], axis=0)
    own_term = jnp.dot(features, self_weight, preferred_element_type=jnp.float32)
    arrived = lax.all_to_all(outgoing, ("graph", "leaf"), split_axis=0, concat_axis=0, tiled=True)
    arrived = arrived.reshape(-1, feat_in)
    picked = jnp.take(arrived, neighbour_slot, axis=0)
    counted = (lax.broadcasted_iota(jnp.int32, neighbour_slot.shape, 1) < degree[:, None]).astype(
        jnp.bfloat16
    )
    summed = jnp.einsum("rk,rkf->rf", counted, picked, preferred_element_type=jnp.float32)
    neigh_mean = (summed / degree[:, None].astype(jnp.float32)).astype(jnp.bfloat16)
    neigh_term = jnp.dot(neigh_mean, neigh_weight, preferred_element_type=jnp.float32)
    hidden = jax.nn.relu(own_term + neigh_term + hidden_bias).astype(jnp.bfloat16)
    raw_embed = jnp.dot(hidden, out_weight, preferred_element_type=jnp.float32) + out_bias
    scaled = raw_embed * lax.rsqrt(
        jnp.mean(raw_embed * raw_embed, axis=1, keepdims=True) + NORM_EPS
    )
    embedded = (scaled * out_gain).astype(jnp.bfloat16)
    vectors = jnp.concatenate([features, embedded], axis=1)
    partial_scores = tree_sums(
        lax.all_gather(vectors, "leaf", axis=0, tiled=True), split_feature, threshold, leaf_value
    )
    scores = lax.psum_scatter(partial_scores, "leaf", scatter_dimension=0, tiled=True)
    return (embedded, scores)


def solution(mesh):
    in_specs = (
        P(("graph", "leaf"), None),
        P(("graph", "leaf"), None, None),
        P(("graph", "leaf"), None),
        P(("graph", "leaf")),
        P(),
        P(),
        P(),
        P(),
        P(),
        P(),
        P("leaf", None),
        P("leaf", None),
        P("leaf", None),
    )
    out_specs = (P(("graph", "leaf"), None), P(("graph", "leaf")))
    return jax.shard_map(
        on_device, mesh=mesh, in_specs=in_specs, out_specs=out_specs, check_vma=False
    )
```

profile of v0, /device:TPU:1, one launch (start us, length us, event | category | flops | bytes accessed | tf_op | source)
XLA Modules:
  0.0 381.4 jit_solution(16077016920772303018)
XLA Ops:
  9.0 17.1 %gather_fusion = bf16[4096,384]{1,0:T(8,128)(2,1)} fusion(bf16[256,384]{1,0:T(8,128)(2,1)S(1)} %copy-done.1, s32[4096]{0:T(1024)S(1)} %broadcast_clamp_fusion.1), kind=kCustom, calls=%fused_computation | custom fusion | bytes 6307840 | tf_op jit(solution)/shard_map/jit(_take)/gather | solution.py:65
  26.2 3.4 broadcast_select_fusion
  29.6 11.9 %all-to-all-start = ((bf16[128,32,384]{2,1,0:T(8,128)(2,1)}), bf16[128,32,384]{2,1,0:T(8,128)(2,1)}, u32[]{:S(2)}, u32[]{:S(2)}) async-start(bf16[128,32,384]{2,1,0:T(8,128)(2,1)} %broadcast_select_fusion), calls=%async_computation | async-start | bytes 6291456 | tf_op jit(solution)/shard_map/all_to_all | solution.py:67
  42.4 40.5 %all-to-all-done = bf16[128,32,384]{2,1,0:T(8,128)(2,1)} async-done(((bf16[128,32,384]{2,1,0:T(8,128)(2,1)}), bf16[128,32,384]{2,1,0:T(8,128)(2,1)}, u32[]{:S(2)}, u32[]{:S(2)}) %all-to-all-start) | async-done | bytes 3145760 | tf_op jit(solution)/shard_map/all_to_all | solution.py:67
  82.9 19.1 %gather_fusion.1 = bf16[4096,384]{1,0:T(8,128)(2,1)} fusion(bf16[4096,384]{1,0:T(8,128)(2,1)} %bitcast.4, s32[4096]{0:T(1024)S(1)} %broadcast_clamp_fusion), kind=kCustom, calls=%fused_computation.1 | custom fusion | bytes 6307840 | tf_op jit(solution)/shard_map/jit(_take)/gather | solution.py:69
  107.7 20.6 %all-gather.2.cloned.1.call-done = bf16[2048,448]{1,0:T(8,128)(2,1)} async-done(((bf16[256,448]{1,0:T(8,128)(2,1)}), bf16[2048,448]{1,0:T(8,128)(2,1)}) %all-gather.2.cloned.1.call-update) | async-done | bytes 1835024 | tf_op jit(solution)/shard_map/all_gather | solution.py:84
  128.3 233.4 %while.11 = (s32[]{:T(128)}, f32[2048]{0:T(1024)S(1)}, s32[8,512]{1,0:T(8,128)S(1)}, bf16[2048,448]{1,0:T(8,128)(2,1)}, f32[8,512]{1,0:T(8,128)S(1)}, /*index=5*/f32[8,8,64]{2,1,0:T(8,128)}, s32[]{:T(128)}, s32[]{:T(128)}) while((s32[]{:T(128)}, f32[2048]{0:T(1024)S(1)}, s32[8,512]{1,0:T(8,128)S(1)}, bf16[2048,448]{1,0:T(8,128)(2,1)}, ...), condition=%wide.region_3.4_spmd.clone, body=%wide.region_1.3_spmd.clone.sunk | while | flops 963758080 | bytes 67102852 | solution.py:46
  128.3 3.1 subtract_multiply_fusion.2
  140.9 2.7 fusion.84
  148.0 6.4 %fusion.85 = (f32[2048,8,32,1]{0,2,1,3:T(8,128)S(1)}, f32[2048,8,32,1]{0,2,1,3:T(8,128)}) fusion(f32[2048,8,32]{0,2,1:T(8,128)} %reshape.129, f32[2048,8,64]{0,2,1:T(8,128)} %bitcast.103), kind=kLoop, calls=%fused_computation.13.clone.1 | loop fusion | flops 8912896 | bytes 8388608 | tf_op jit(solution)/shard_map/while/body/eval_jaxpr/stack | solution.py:35
  157.5 3.1 subtract_multiply_fusion.2
  170.1 2.7 fusion.84
  177.2 6.4 %fusion.85 = (f32[2048,8,32,1]{0,2,1,3:T(8,128)S(1)}, f32[2048,8,32,1]{0,2,1,3:T(8,128)}) fusion(f32[2048,8,32]{0,2,1:T(8,128)} %reshape.129, f32[2048,8,64]{0,2,1:T(8,128)} %bitcast.103), kind=kLoop, calls=%fused_computation.13.clone.1 | loop fusion | flops 8912896 | bytes 8388608 | tf_op jit(solution)/shard_map/while/body/eval_jaxpr/stack | solution.py:35
  186.7 3.1 subtract_multiply_fusion.2
  199.3 2.7 fusion.84
  206.4 6.4 %fusion.85 = (f32[2048,8,32,1]{0,2,1,3:T(8,128)S(1)}, f32[2048,8,32,1]{0,2,1,3:T(8,128)}) fusion(f32[2048,8,32]{0,2,1:T(8,128)} %reshape.129, f32[2048,8,64]{0,2,1:T(8,128)} %bitcast.103), kind=kLoop, calls=%fused_computation.13.clone.1 | loop fusion | flops 8912896 | bytes 8388608 | tf_op jit(solution)/shard_map/while/body/eval_jaxpr/stack | solution.py:35
  215.8 3.1 subtract_multiply_fusion.2
  228.4 2.7 fusion.84
  235.5 6.4 %fusion.85 = (f32[2048,8,32,1]{0,2,1,3:T(8,128)S(1)}, f32[2048,8,32,1]{0,2,1,3:T(8,128)}) fusion(f32[2048,8,32]{0,2,1:T(8,128)} %reshape.129, f32[2048,8,64]{0,2,1:T(8,128)} %bitcast.103), kind=kLoop, calls=%fused_computation.13.clone.1 | loop fusion | flops 8912896 | bytes 8388608 | tf_op jit(solution)/shard_map/while/body/eval_jaxpr/stack | solution.py:35
  245.0 3.1 subtract_multiply_fusion.2
  257.6 2.7 fusion.84
  264.7 6.4 %fusion.85 = (f32[2048,8,32,1]{0,2,1,3:T(8,128)S(1)}, f32[2048,8,32,1]{0,2,1,3:T(8,128)}) fusion(f32[2048,8,32]{0,2,1:T(8,128)} %reshape.129, f32[2048,8,64]{0,2,1:T(8,128)} %bitcast.103), kind=kLoop, calls=%fused_computation.13.clone.1 | loop fusion | flops 8912896 | bytes 8388608 | tf_op jit(solution)/shard_map/while/body/eval_jaxpr/stack | solution.py:35
  274.2 3.1 subtract_multiply_fusion.2
  286.8 2.7 fusion.84
  293.9 6.4 %fusion.85 = (f32[2048,8,32,1]{0,2,1,3:T(8,128)S(1)}, f32[2048,8,32,1]{0,2,1,3:T(8,128)}) fusion(f32[2048,8,32]{0,2,1:T(8,128)} %reshape.129, f32[2048,8,64]{0,2,1:T(8,128)} %bitcast.103), kind=kLoop, calls=%fused_computation.13.clone.1 | loop fusion | flops 8912896 | bytes 8388608 | tf_op jit(solution)/shard_map/while/body/eval_jaxpr/stack | solution.py:35
  303.4 3.1 subtract_multiply_fusion.2
  315.9 2.7 fusion.84
  323.1 6.4 %fusion.85 = (f32[2048,8,32,1]{0,2,1,3:T(8,128)S(1)}, f32[2048,8,32,1]{0,2,1,3:T(8,128)}) fusion(f32[2048,8,32]{0,2,1:T(8,128)} %reshape.129, f32[2048,8,64]{0,2,1:T(8,128)} %bitcast.103), kind=kLoop, calls=%fused_computation.13.clone.1 | loop fusion | flops 8912896 | bytes 8388608 | tf_op jit(solution)/shard_map/while/body/eval_jaxpr/stack | solution.py:35
  332.5 3.1 subtract_multiply_fusion.2
  345.1 2.7 fusion.84
  352.2 6.4 %fusion.85 = (f32[2048,8,32,1]{0,2,1,3:T(8,128)S(1)}, f32[2048,8,32,1]{0,2,1,3:T(8,128)}) fusion(f32[2048,8,32]{0,2,1:T(8,128)} %reshape.129, f32[2048,8,64]{0,2,1:T(8,128)} %bitcast.103), kind=kLoop, calls=%fused_computation.13.clone.1 | loop fusion | flops 8912896 | bytes 8388608 | tf_op jit(solution)/shard_map/while/body/eval_jaxpr/stack | solution.py:35
  361.7 12.2 %all-reduce.2 = f32[2048]{0:T(1024)S(1)} all-reduce(f32[2048]{0:T(1024)S(1)} %get-tuple-element.39), channel_id=2, replica_groups=mesh['graph'=16,'leaf'=8] {'leaf'}, use_global_device_ids=true, to_apply=%region_4.5.clone | all-reduce | flops 2048 | bytes 16384
  (256 shorter events, 142.7 us)
Async XLA Ops:
  7.2 34.9 %copy-start = (bf16[384,512]{1,0:T(8,128)(2,1)S(1)}, bf16[384,512]{1,0:T(8,128)(2,1)}, u32[]{:S(2)}) copy-start(bf16[384,512]{1,0:T(8,128)(2,1)} %param.19) | copy-start | bytes 1179652
  7.2 1.8 copy-start.1
  29.6 12.0 %copy-start.4 = (s32[256,16]{0,1:T(8,128)S(1)}, s32[256,16]{0,1:T(8,128)}, u32[]{:S(2)}) copy-start(s32[256,16]{0,1:T(8,128)} %param.17) | copy-start | bytes 49156
  29.6 12.3 %copy-start.7 = (s32[256]{0:T(256)S(1)}, s32[256]{0:T(256)}, u32[]{:S(2)}) copy-start(s32[256]{0:T(256)} %param.18) | copy-start | bytes 3076
  29.6 53.3 %all-to-all-start = ((bf16[128,32,384]{2,1,0:T(8,128)(2,1)}), bf16[128,32,384]{2,1,0:T(8,128)(2,1)}, u32[]{:S(2)}, u32[]{:S(2)}) async-start(bf16[128,32,384]{2,1,0:T(8,128)(2,1)} %broadcast_select_fusion), calls=%async_computation | async-start | bytes 6291456 | tf_op jit(solution)/shard_map/all_to_all | solution.py:67
  41.5 86.8 %all-gather.2.cloned.1.call-start = ((), (), s32[]{:S(2)}) async-start(), calls=%async_computation.1 | async-start | bytes 2359296 | tf_op jit(solution)/shard_map/all_gather | solution.py:84
  102.0 2.6 copy-start.9
  102.0 2.6 copy-start.10
  102.0 2.7 copy-start.11
  102.0 2.7 copy-start.12
  104.7 0.7 copy-start.8
  104.7 1.6 copy-start.5
  104.7 1.7 copy-start.6
  104.7 1.8 copy-start.13
  105.4 22.9 %copy-start.3 = (bf16[256,64]{0,1:T(8,128)(2,1)}, bf16[256,64]{0,1:T(8,128)(2,1)S(1)}, u32[]{:S(2)}) copy-start(bf16[256,64]{0,1:T(8,128)(2,1)S(1)} %multiply_convert_fusion) | copy-start | bytes 98308
  131.4 2.0 copy-start.2
  160.6 2.0 copy-start.2
  189.8 2.0 copy-start.2
  219.0 2.0 copy-start.2
  248.1 2.0 copy-start.2
  277.3 2.0 copy-start.2
  306.5 2.0 copy-start.2
  335.6 2.0 copy-start.2
Sparse Core Ops, SparseCore 0:
  106.4 21.8 all-gather.1
where the time goes:
time: 384 us; the launch traced here: 381 us
  other arithmetic  141 us (37%)
  local copies, waits for them, and re-layouts  111 us (29%)
  waiting for transfers between devices  61.1 us (16%)
  matrix products  28.2 us (7%)
  between operations  14.9 us (4%)
  blocking collectives  12.2 us (3%)
  starting transfers between devices  11.9 us (3%)
    another operation x80, other arithmetic, one_block(): jnp.stack([go_left, go_right], axis=-1)  117 us
    all_to_all x1, waiting for transfers between devices, on_device(): lax.all_to_all(outgoing, ('graph', 'leaf'), split_axis=0, concat_axis=0,...  40.5 us
    reshape x32, local copies, waits for them, and re-layouts, one_block(): jnp.stack([go_left, go_right], axis=-1)  30.5 us
    dot_general x8, matrix products, one_block(): chosen = jnp.dot(card_rows, selector, preferred_element_type=jnp.float32)  24.8 us
    another operation x32, local copies, waits for them, and re-layouts, one_block(): jnp.stack([go_left, go_right], axis=-1)  24.5 us
    all_gather x1, waiting for transfers between devices, on_device(): lax.all_gather(vectors, 'leaf', axis=0, tiled=True)  20.6 us
    gather x1, local copies, waits for them, and re-layouts, on_device(): picked = jnp.take(arrived, neighbour_slot, axis=0)  19.1 us
    reduce_sum x8, other arithmetic, one_block(): added = jnp.sum(jnp.exp(log_reach) * block_scores[None], axis=(1, 2))  17.5 us
  transfers between devices with their start and end apart: 2, of which 2 were waited for; matrix products, arithmetic and copies ran while one was open for 0% of the time, Pallas kernels for 0%

commit v1 on v0

v1 whole, which is shorter than its diff:
```python
import functools

import jax
import jax.numpy as jnp
from jax import lax
from jax.experimental import pallas as pl
from jax.experimental.pallas import tpu as pltpu
from jax.sharding import PartitionSpec as P

NORM_EPS = 1e-05
CAP = 32
GROUP = 16
BF16 = jnp.bfloat16
F32 = jnp.float32
MESH = pl.DeviceIdType.MESH


def post_order(inner):
    order = []

    def visit(node):
        if node < inner:
            visit(2 * node + 1)
            visit(2 * node + 2)
            order.append(node)

    visit(0)
    place = [0] * inner
    for position, node in enumerate(order):
        place[node] = position
    return place


def flip(a, b, size):
    total = 0
    bit = 1
    while bit < size:
        total = total + ((a // bit + b // bit) % 2) * bit
        bit *= 2
    return total


def kernel(
    graphs,
    leaves,
    features,
    send_rows,
    neighbour_slot,
    degree,
    self_weight,
    neigh_weight,
    hidden_bias,
    out_weight,
    out_bias,
    out_gain,
    split_feature,
    threshold,
    leaf_value,
    embedding,
    scores,
    feats,
    ids,
    outgoing,
    arrived,
    slot_ids,
    counts,
    selector,
    leaf_mid,
    leaf_half,
    inputs_t,
    own_term,
    out_weight_t,
    out_cols,
    degree_col,
    summed,
    partial,
    partial_in,
    feat_send,
    ids_send,
    row_send,
    emb_send,
    score_send,
    feat_recv,
    ids_recv,
    row_recv,
    emb_recv,
    score_recv,
):
    g = lax.axis_index("graph")
    m = lax.axis_index("leaf")
    rows, f_in = features.shape
    trees, inner = split_feature.shape
    emb = out_weight.shape[1]
    entries = neighbour_slot.shape[1]
    width = leaves * CAP
    groups = trees // GROUP
    place = post_order(inner)
    lanes = lax.broadcasted_iota(jnp.int32, (1, 128), 1)

    barrier = pltpu.get_barrier_semaphore()

    @pl.loop(1, graphs)
    def _(step):
        pl.semaphore_signal(
            barrier, inc=1, device_id=(lax.rem(g + step, graphs), m), device_id_type=MESH
        )

    @pl.loop(1, leaves)
    def _(step):
        pl.semaphore_signal(
            barrier, inc=1, device_id=(g, flip(m, step, leaves)), device_id_type=MESH
        )

    devices = graphs * leaves
    wide = jnp.concatenate([send_rows[...], jnp.zeros((devices, 128 - CAP), jnp.int32)], axis=1)
    ids[0] = wide.T[:CAP]
    feats[0] = features[...]
    pl.semaphore_wait(barrier, graphs - 1 + leaves - 1)

    def leaf_order(i):
        if leaves == 8:
            return i + 2 * ((i // 4) * (1 - 2 * ((i // 2) % 2)))
        return i

    @pl.loop(1, leaves)
    def _(i):
        p = leaf_order(i)
        peer = (g, flip(m, p, leaves))
        pltpu.make_async_remote_copy(
            src_ref=ids.at[0], dst_ref=ids.at[p], send_sem=ids_send, recv_sem=ids_recv.at[p],
            device_id=peer, device_id_type=MESH,
        ).start()
        pltpu.make_async_remote_copy(
            src_ref=feats.at[0], dst_ref=feats.at[p], send_sem=feat_send, recv_sem=feat_recv.at[p],
            device_id=peer, device_id_type=MESH,
        ).start()

    row_lanes = lax.broadcasted_iota(jnp.int32, (1, rows), 1)

    def gather_one(p):
        if not isinstance(p, int) or p > 0:
            pltpu.make_async_copy(ids.at[p], ids.at[p], ids_recv.at[p]).wait()
            pltpu.make_async_copy(feats.at[p], feats.at[p], feat_recv.at[p]).wait()
        mine = pltpu.roll(ids[p], devices - m, axis=1)
        pieces = []
        for target in range(graphs):
            column = mine[:, target * leaves : target * leaves + 1]
            pieces.append((column == row_lanes).astype(F32).astype(BF16))
        picked = jnp.dot(
            jnp.concatenate(pieces, axis=0), feats[p], preferred_element_type=F32
        ).astype(BF16)
        for target in range(graphs):
            outgoing[target, pl.ds(p * CAP, CAP), :] = picked[target * CAP : (target + 1) * CAP]
        inputs_t[p, 0:f_in, :] = feats[p].T

    def send_pair(first):
        @pl.loop(1, graphs)
        def _(step):
            target = lax.rem(g + step, graphs)
            part = pl.ds(first * CAP, 2 * CAP)
            pltpu.make_async_remote_copy(
                src_ref=outgoing.at[target, part],
                dst_ref=arrived.at[g, part],
                send_sem=row_send,
                recv_sem=row_recv.at[g],
                device_id=(target, m),
                device_id_type=MESH,
            ).start()

    def build_selector():
        @pl.loop(0, groups)
        def _(tg):
            base = pl.multiple_of(tg * GROUP, GROUP)
            node_ids = split_feature[pl.ds(base, GROUP), :]
            cuts = threshold[pl.ds(base, GROUP), :]
            high = cuts.astype(BF16).astype(F32)
            middle = (cuts - high).astype(BF16).astype(F32)
            low = cuts - high - middle
            for node in range(inner):
                column = jnp.broadcast_to(node_ids[:, node : node + 1], (GROUP, 128))
                parts = []
                for q in range(4):
                    parts.append(jnp.where(column == lanes + q * 128, 1.0, 0.0))
                last = parts[3]
                for extra, part in enumerate((high, middle, low)):
                    last = jnp.where(lanes == 64 + extra, -part[:, node : node + 1], last)
                parts[3] = last
                selector[tg, place[node] * GROUP : (place[node] + 1) * GROUP, :] = jnp.concatenate(
                    parts, axis=1
                ).astype(BF16)
            values = leaf_value[pl.ds(base, GROUP), :]
            for pair in range((inner + 1) // 2):
                left = values[:, 2 * pair : 2 * pair + 1]
                right = values[:, 2 * pair + 1 : 2 * pair + 2]
                where = slice(pair * GROUP, (pair + 1) * GROUP)
                scale = 1.0 / (inner + 1)
                leaf_mid[tg, where, :] = jnp.broadcast_to((left + right) * scale, (GROUP, 128))
                leaf_half[tg, where, :] = jnp.broadcast_to((right - left) * scale, (GROUP, 128))

    def build_counts():
        degrees = jnp.broadcast_to(degree[...].astype(F32), (128, rows)).T
        degree_col[...] = degrees
        for j in range(entries):
            named = jnp.broadcast_to(neighbour_slot[:, j : j + 1], (rows, 128)) ^ (m * CAP)
            slot_ids[j] = jnp.where(degrees > j + 0.5, named, -1)

        @pl.loop(0, graphs)
        def _(source):
            for half in range(width // 128):
                here = lanes + (source * width + half * 128)
                for part in range(0, rows, 128):
                    total = jnp.zeros((128, 128), F32)
                    for j in range(entries):
                        total = total + jnp.where(slot_ids[j, part : part + 128] == here, 1.0, 0.0)
                    counts[source, part : part + 128, half * 128 : (half + 1) * 128] = total.astype(
                        BF16
                    )

    def build_rest():
        own_term[...] = (
            jnp.dot(features[...], self_weight[...], preferred_element_type=F32) + hidden_bias[...]
        )
        padded = jnp.concatenate(
            [out_weight[...].astype(F32), jnp.zeros((out_weight.shape[0], 128 - emb), F32)], axis=1
        )
        out_weight_t[...] = padded.T[:emb].astype(BF16)
        for place_at, row in enumerate((out_bias, out_gain)):
            wide_row = jnp.concatenate([row[...], jnp.zeros((1, 128 - emb), F32)], axis=1)
            out_cols[place_at] = jnp.broadcast_to(wide_row, (128, 128)).T[:emb]
        for p in range(leaves):
            inputs_t[p, f_in + emb :, :] = jnp.ones((512 - f_in - emb, rows), BF16)

    pair_order = (0, 2, 6, 4) if leaves == 8 else tuple(range(0, leaves, 2))
    fillers = [build_selector, build_rest, build_counts]
    for at, first in enumerate(pair_order):
        gather_one(first)
        gather_one(first + 1)
        send_pair(first)
        if at < len(fillers):
            fillers[at]()
    for filler in fillers[len(pair_order) :]:
        filler()

    summed[...] = jnp.dot(counts[g], outgoing[g], preferred_element_type=F32)

    @pl.loop(1, graphs)
    def _(step):
        source = lax.rem(g + graphs - step, graphs)
        pltpu.make_async_copy(
            arrived.at[source], arrived.at[source], row_recv.at[source]
        ).wait()
        summed[...] += jnp.dot(counts[source], arrived[source], preferred_element_type=F32)

    by = jnp.concatenate([degree_col[...]] * (f_in // 128), axis=1)
    mean = (summed[...] / by).astype(BF16)
    hidden = jnp.maximum(
        own_term[...] + jnp.dot(mean, neigh_weight[...], preferred_element_type=F32), 0.0
    ).astype(BF16)
    across = rows // 128
    raw = lax.dot_general(
        out_weight_t[...], hidden, (((1,), (1,)), ((), ())), preferred_element_type=F32
    ) + jnp.concatenate([out_cols[0]] * across, axis=1)
    level = lax.rsqrt(jnp.sum(raw * raw, axis=0, keepdims=True) * (1.0 / emb) + NORM_EPS)
    made_t = raw * level * jnp.concatenate([out_cols[1]] * across, axis=1)
    inputs_t[0, f_in : f_in + emb, :] = made_t.astype(BF16)

    @pl.loop(1, leaves)
    def _(i):
        p = leaf_order(i)
        part = pl.ds(f_in, emb)
        pltpu.make_async_remote_copy(
            src_ref=inputs_t.at[0, part], dst_ref=inputs_t.at[p, part], send_sem=emb_send,
            recv_sem=emb_recv.at[p], device_id=(g, flip(m, p, leaves)), device_id_type=MESH,
        ).start()

    made = jnp.concatenate([made_t, jnp.zeros((128 - emb, rows), F32)], axis=0).T
    embedding[...] = made[:, :emb].astype(BF16)

    def one_group(p, tg, column):
        margin = jnp.dot(selector[tg], inputs_t[p], preferred_element_type=F32)

        def value(node, half):
            at = place[node] * GROUP
            if 2 * node + 1 >= inner:
                pair = node - inner // 2
                low = leaf_mid[tg, pair * GROUP : (pair + 1) * GROUP, :]
                gap = leaf_half[tg, pair * GROUP : (pair + 1) * GROUP, :]
            else:
                left = value(2 * node + 1, half)
                right = value(2 * node + 2, half)
                low = left + right
                gap = right - left
            turn = jnp.tanh(margin[at : at + GROUP, half * 128 : (half + 1) * 128])
            return low + turn * gap

        for half in range(rows // 128):
            total = value(0, half)
            where = slice(half * 128, (half + 1) * 128)
            partial[column, :, where] += total[:8] + total[8:]

    @pl.loop(0, leaves)
    def _(i):
        p = leaf_order(i)

        @pl.when(i > 0)
        def _():
            part = inputs_t.at[p, pl.ds(f_in, emb)]
            pltpu.make_async_copy(part, part, emb_recv.at[p]).wait()

        partial[p] = jnp.zeros(partial.shape[1:], F32)

        @pl.loop(0, groups)
        def _(tg):
            one_group(p, tg, p)

        @pl.when(i > 0)
        def _():
            pltpu.make_async_remote_copy(
                src_ref=partial.at[p], dst_ref=partial_in.at[p], send_sem=score_send,
                recv_sem=score_recv.at[p], device_id=(g, flip(m, p, leaves)), device_id_type=MESH,
            ).start()

    running = partial[0]
    for p in range(1, leaves):
        pltpu.make_async_copy(partial_in.at[p], partial_in.at[p], score_recv.at[p]).wait()
        running = running + partial_in[p]
    scores[...] = jnp.sum(running, axis=0, keepdims=True)

    others = pl.ds(0, leaves - 1)
    pltpu.make_async_copy(ids.at[others], ids.at[others], ids_send).wait()
    pltpu.make_async_copy(feats.at[others], feats.at[others], feat_send).wait()
    block = outgoing.at[pl.ds(0, graphs - 1)]
    pltpu.make_async_copy(block, block, row_send).wait()
    block = inputs_t.at[others, pl.ds(f_in, emb)]
    pltpu.make_async_copy(block, block, emb_send).wait()
    pltpu.make_async_copy(partial.at[others], partial.at[others], score_send).wait()


def on_device(
    graphs,
    leaves,
    features,
    send_rows,
    neighbour_slot,
    degree,
    self_weight,
    neigh_weight,
    hidden_bias,
    out_weight,
    out_bias,
    out_gain,
    split_feature,
    threshold,
    leaf_value,
):
    rows, f_in = features.shape
    hid = self_weight.shape[1]
    emb = out_weight.shape[1]
    trees, inner = split_feature.shape
    groups = trees // GROUP
    width = leaves * CAP
    entries = neighbour_slot.shape[1]
    dma = pltpu.SemaphoreType.DMA
    vmem = pl.BlockSpec(memory_space=pltpu.VMEM)
    embedding, scores = pl.pallas_call(
        functools.partial(kernel, graphs, leaves),
        out_shape=(
            jax.ShapeDtypeStruct((rows, emb), BF16),
            jax.ShapeDtypeStruct((1, rows), F32),
        ),
        in_specs=[vmem] * 13,
        out_specs=(vmem, vmem),
        scratch_shapes=[
            pltpu.VMEM((leaves, rows, f_in), BF16),
            pltpu.VMEM((leaves, CAP, graphs * leaves), jnp.int32),
            pltpu.VMEM((graphs, width, f_in), BF16),
            pltpu.VMEM((graphs, width, f_in), BF16),
            pltpu.VMEM((entries, rows, 128), jnp.int32),
            pltpu.VMEM((graphs, rows, width), BF16),
            pltpu.VMEM((groups, inner * GROUP, 512), BF16),
            pltpu.VMEM((groups, (inner + 1) // 2 * GROUP, 128), F32),
            pltpu.VMEM((groups, (inner + 1) // 2 * GROUP, 128), F32),
            pltpu.VMEM((leaves, 512, rows), BF16),
            pltpu.VMEM((rows, hid), F32),
            pltpu.VMEM((emb, hid), BF16),
            pltpu.VMEM((2, emb, 128), F32),
            pltpu.VMEM((rows, 128), F32),
            pltpu.VMEM((rows, f_in), F32),
            pltpu.VMEM((leaves, 8, rows), F32),
            pltpu.VMEM((leaves, 8, rows), F32),
            dma,
            dma,
            dma,
            dma,
            dma,
            dma((leaves,)),
            dma((leaves,)),
            dma((graphs,)),
            dma((leaves,)),
            dma((leaves,)),
        ],
        compiler_params=pltpu.CompilerParams(
            collective_id=0, has_side_effects=True, vmem_limit_bytes=56 * 2**20
        ),
        name="sage_forest",
    )(
        features,
        send_rows.reshape(send_rows.shape[1:]),
        neighbour_slot,
        degree.reshape(1, rows),
        self_weight,
        neigh_weight,
        hidden_bias.reshape(1, hid),
        out_weight,
        out_bias.reshape(1, emb),
        out_gain.reshape(1, emb),
        split_feature,
        threshold,
        leaf_value,
    )
    return (embedding, scores.reshape(rows))


def solution(mesh):
    in_specs = (
        P(("graph", "leaf"), None),
        P(("graph", "leaf"), None, None),
        P(("graph", "leaf"), None),
        P(("graph", "leaf")),
        P(),
        P(),
        P(),
        P(),
        P(),
        P(),
        P("leaf", None),
        P("leaf", None),
        P("leaf", None),
    )
    out_specs = (P(("graph", "leaf"), None), P(("graph", "leaf")))
    return jax.shard_map(
        functools.partial(on_device, mesh.shape["graph"], mesh.shape["leaf"]),
        mesh=mesh,
        in_specs=in_specs,
        out_specs=out_specs,
        check_vma=False,
    )
```

time: 384 us -> 78.5 us (0.20)
  other arithmetic: 141 us -> 0 us
  local copies, waits for them, and re-layouts: 111 us -> 5.81 us
  Pallas kernels: 0 us -> 71.7 us
  waiting for transfers between devices: 61.1 us -> 0 us
  matrix products: 28.2 us -> 0 us
  between operations: 14.9 us -> 0.65 us
  blocking collectives: 12.2 us -> 0 us
  starting transfers between devices: 11.9 us -> 0 us
    another operation x80 -> x0, other arithmetic: 117 us -> none  [one_block(): jnp.stack([go_left, go_right], axis=-1)]
    pallas_call x0 -> x1, Pallas kernels: none -> 71.7 us  [on_device(): pl.pallas_call(functools.partial(kernel, graphs, leaves), out_shape=(jax....]
    all_to_all x1 -> x0, waiting for transfers between devices: 40.5 us -> none  [on_device(): lax.all_to_all(outgoing, ('graph', 'leaf'), split_axis=0, concat_axis=0,...]
    gather x2 -> x0, local copies, waits for them, and re-layouts: 36.2 us -> none  [the longest x1 19.1 us: on_device(): picked = jnp.take(arrived, neighbour_slot, axis=0)]
    reshape x34 -> x0, local copies, waits for them, and re-layouts: 30.6 us -> none  [the longest x32 30.5 us: one_block(): jnp.stack([go_left, go_right], axis=-1)]
    dot_general x11 -> x0, matrix products: 28.2 us -> none  [the longest x8 24.8 us: one_block(): chosen = jnp.dot(card_rows, selector, preferred_element_type=jnp.float32)]
    another operation x32 -> x0, local copies, waits for them, and re-layouts: 24.5 us -> none  [one_block(): jnp.stack([go_left, go_right], axis=-1)]
    all_gather x1 -> x0, waiting for transfers between devices: 20.6 us -> none  [on_device(): lax.all_gather(vectors, 'leaf', axis=0, tiled=True)]
  transfers between devices with their start and end apart: 2 -> 0, of which waited for: 2 -> 0; matrix products, arithmetic and copies ran while one was open for 0% -> 0% of each run, Pallas kernels for 0% -> 0%
where the time goes in v1:
time: 78.5 us; the launch traced here: 78.2 us
  Pallas kernels  71.7 us (91%)
  local copies, waits for them, and re-layouts  5.81 us (7%)
    pallas_call x1, Pallas kernels, on_device(): pl.pallas_call(functools.partial(kernel, graphs, leaves), out_shape=(jax....  71.7 us
    unnamed x11, local copies, waits for them, and re-layouts  5.81 us

profile of v1, /device:TPU:1, one launch (start us, length us, event | category | flops | bytes accessed | tf_op | source)
XLA Modules:
  0.0 78.2 jit_solution(11371868977417752300)
XLA Ops:
  0.6 0.0 copy-start.1
  0.6 1.5 %copy.15 = s32[1,128,32]{2,1,0:T(8,128)} copy(s32[1,128,32]{1,2,0:T(8,128)} %param.14) | data formatting | bytes 32768 | tf_op args[1]
  2.1 0.0 copy-done.1
  2.1 0.0 copy-start
  2.1 0.7 copy.16.neighbour_slot
  2.8 0.1 copy-done
  2.9 0.7 copy.17.out_weight
  3.7 71.7 %sage_forest.1 = (bf16[256,64]{1,0:T(8,128)(2,1)}, f32[1,256]{1,0:T(1,128)}) custom-call(bf16[256,384]{1,0:T(8,128)(2,1)} %features.1, s32[128,32]{1,0:T(8,128)} %bitcast.6, s32[256,16]{1,0:T(8,128)} %copy.16.neighbour_slot, s32[1,256]{1,0:T(1,128)} %bitcast.9, bf16[384,512]{1,0:T(8,128)(2,1)} %self_weight.1, bf16[384,512]{1,0:T(8,128)(2,1)} %neigh_weight.1, ...), custom_call_target="tpu_custom_call" | custom-call | tf_op jit(solution)/shard_map/sage_forest/pallas_call | solution.py:365
  75.4 1.5 %copy.18 = bf16[256,64]{0,1:T(8,128)(2,1)} copy(bf16[256,64]{1,0:T(8,128)(2,1)} %get-tuple-element.6) | data formatting | bytes 65536
  77.0 0.0 copy-start.2
  77.0 0.7 copy-done.2
  77.6 0.6 copy.20
Async XLA Ops:
  0.6 1.5 %copy-start.1 = (s32[256,16]{0,1:T(8,128)S(1)}, s32[256,16]{0,1:T(8,128)}, u32[]{:S(2)}) copy-start(s32[256,16]{0,1:T(8,128)} %param.15) | copy-start | bytes 49156
  2.1 0.8 %copy-start = (bf16[512,64]{0,1:T(8,128)(2,1)S(1)}, bf16[512,64]{0,1:T(8,128)(2,1)}, u32[]{:S(2)}) copy-start(bf16[512,64]{0,1:T(8,128)(2,1)} %param.20) | copy-start | bytes 196612
  77.0 0.7 copy-start.2

commit v2 on v1

--- a/solution.py
+++ b/solution.py
@@ -50,13 +50,13 @@
     self_weight,
     neigh_weight,
     hidden_bias,
-    out_weight,
+    out_weight_t,
     out_bias,
     out_gain,
     split_feature,
     threshold,
     leaf_value,
-    embedding,
+    embedding_t,
     scores,
     feats,
     ids,
@@ -67,9 +67,10 @@
     selector,
     leaf_mid,
     leaf_half,
-    inputs_t,
+    feat_t,
+    emb_t,
+    margins,
     own_term,
-    out_weight_t,
     out_cols,
     degree_col,
     summed,
@@ -90,8 +91,8 @@
     m = lax.axis_index("leaf")
     rows, f_in = features.shape
     trees, inner = split_feature.shape
-    emb = out_weight.shape[1]
-    entries = neighbour_slot.shape[1]
+    emb = out_weight_t.shape[0]
+    entries = neighbour_slot.shape[0]
     width = leaves * CAP
     groups = trees // GROUP
     place = post_order(inner)
@@ -112,35 +113,32 @@
         )
 
     devices = graphs * leaves
-    wide = jnp.concatenate([send_rows[...], jnp.zeros((devices, 128 - CAP), jnp.int32)], axis=1)
-    ids[0] = wide.T[:CAP]
+    ids[0] = send_rows[...]
     feats[0] = features[...]
-    pl.semaphore_wait(barrier, graphs - 1 + leaves - 1)
 
     def leaf_order(i):
         if leaves == 8:
             return i + 2 * ((i // 4) * (1 - 2 * ((i // 2) % 2)))
         return i
 
-    @pl.loop(1, leaves)
-    def _(i):
-        p = leaf_order(i)
-        peer = (g, flip(m, p, leaves))
+    def send_feats(source, p):
         pltpu.make_async_remote_copy(
-            src_ref=ids.at[0], dst_ref=ids.at[p], send_sem=ids_send, recv_sem=ids_recv.at[p],
-            device_id=peer, device_id_type=MESH,
+            src_ref=feats.at[source],
+            dst_ref=feats.at[flip(source, p, leaves)],
+            send_sem=feat_send,
+            recv_sem=feat_recv.at[flip(source, p, leaves)],
+            device_id=(g, flip(m, p, leaves)),
+            device_id_type=MESH,
         ).start()
-        pltpu.make_async_remote_copy(
-            src_ref=feats.at[0], dst_ref=feats.at[p], send_sem=feat_send, recv_sem=feat_recv.at[p],
-            device_id=peer, device_id_type=MESH,
-        ).start()
 
     row_lanes = lax.broadcasted_iota(jnp.int32, (1, rows), 1)
 
     def gather_one(p):
-        if not isinstance(p, int) or p > 0:
+        if p > 0:
             pltpu.make_async_copy(ids.at[p], ids.at[p], ids_recv.at[p]).wait()
             pltpu.make_async_copy(feats.at[p], feats.at[p], feat_recv.at[p]).wait()
+            if p % 2 == 0:
+                send_feats(p, 1)
         mine = pltpu.roll(ids[p], devices - m, axis=1)
         pieces = []
         for target in range(graphs):
@@ -151,13 +149,12 @@
         ).astype(BF16)
         for target in range(graphs):
             outgoing[target, pl.ds(p * CAP, CAP), :] = picked[target * CAP : (target + 1) * CAP]
-        inputs_t[p, 0:f_in, :] = feats[p].T
-
-    def send_pair(first):
+
+    def send_part(p):
         @pl.loop(1, graphs)
         def _(step):
             target = lax.rem(g + step, graphs)
-            part = pl.ds(first * CAP, 2 * CAP)
+            part = pl.ds(p * CAP, CAP)
             pltpu.make_async_remote_copy(
                 src_ref=outgoing.at[target, part],
                 dst_ref=arrived.at[g, part],
@@ -200,8 +197,11 @@
     def build_counts():
         degrees = jnp.broadcast_to(degree[...].astype(F32), (128, rows)).T
         degree_col[...] = degrees
+        named_all = jnp.concatenate(
+            [neighbour_slot[...], jnp.zeros((128 - entries, rows), jnp.int32)], axis=0
+        ).T ^ (m * CAP)
         for j in range(entries):
-            named = jnp.broadcast_to(neighbour_slot[:, j : j + 1], (rows, 128)) ^ (m * CAP)
+            named = jnp.broadcast_to(named_all[:, j : j + 1], (rows, 128))
             slot_ids[j] = jnp.where(degrees > j + 0.5, named, -1)
 
         @pl.loop(0, graphs)
@@ -220,35 +220,57 @@
         own_term[...] = (
             jnp.dot(features[...], self_weight[...], preferred_element_type=F32) + hidden_bias[...]
         )
-        padded = jnp.concatenate(
-            [out_weight[...].astype(F32), jnp.zeros((out_weight.shape[0], 128 - emb), F32)], axis=1
-        )
-        out_weight_t[...] = padded.T[:emb].astype(BF16)
         for place_at, row in enumerate((out_bias, out_gain)):
             wide_row = jnp.concatenate([row[...], jnp.zeros((1, 128 - emb), F32)], axis=1)
             out_cols[place_at] = jnp.broadcast_to(wide_row, (128, 128)).T[:emb]
-        for p in range(leaves):
-            inputs_t[p, f_in + emb :, :] = jnp.ones((512 - f_in - emb, rows), BF16)
+        for pair in range(leaves // 2):
+            emb_t[pair, emb:, :] = jnp.ones((128 - emb, 2 * rows), BF16)
+
+    def build_margins():
+        @pl.loop(0, leaves // 2)
+        def _(pair):
+            for core in range(2):
+                feat_t[:, core * rows : (core + 1) * rows] = feats[2 * pair + core].T
+
+            @pl.loop(0, groups)
+            def _(tg):
+                margins[pair, tg] = jnp.dot(
+                    selector[tg, :, :f_in], feat_t[...], preferred_element_type=F32
+                )
 
     pair_order = (0, 2, 6, 4) if leaves == 8 else tuple(range(0, leaves, 2))
-    fillers = [build_selector, build_rest, build_counts]
-    for at, first in enumerate(pair_order):
-        gather_one(first)
-        gather_one(first + 1)
-        send_pair(first)
-        if at < len(fillers):
-            fillers[at]()
-    for filler in fillers[len(pair_order) :]:
-        filler()
+    gather_one(0)
+    pl.semaphore_wait(barrier, graphs - 1 + leaves - 1)
+
+    @pl.loop(1, leaves)
+    def _(i):
+        p = leaf_order(i)
+        pltpu.make_async_remote_copy(
+            src_ref=ids.at[0], dst_ref=ids.at[p], send_sem=ids_send, recv_sem=ids_recv.at[p],
+            device_id=(g, flip(m, p, leaves)), device_id_type=MESH,
+        ).start()
+
+    for p in (1,) + pair_order[1:]:
+        send_feats(0, p)
+    send_part(0)
+    gather_one(1)
+    send_part(1)
+    build_selector()
+    for at, first in enumerate(pair_order[1:]):
+        for p in (first, first + 1):
+            gather_one(p)
+            send_part(p)
+        if at == 0:
+            build_rest()
+    build_counts()
+    build_margins()
 
     summed[...] = jnp.dot(counts[g], outgoing[g], preferred_element_type=F32)
 
     @pl.loop(1, graphs)
     def _(step):
         source = lax.rem(g + graphs - step, graphs)
-        pltpu.make_async_copy(
-            arrived.at[source], arrived.at[source], row_recv.at[source]
-        ).wait()
+        pltpu.make_async_copy(arrived.at[source], arrived.at[source], row_recv.at[source]).wait()
         summed[...] += jnp.dot(counts[source], arrived[source], preferred_element_type=F32)
 
     by = jnp.concatenate([degree_col[...]] * (f_in // 128), axis=1)
@@ -262,64 +284,81 @@
     ) + jnp.concatenate([out_cols[0]] * across, axis=1)
     level = lax.rsqrt(jnp.sum(raw * raw, axis=0, keepdims=True) * (1.0 / emb) + NORM_EPS)
     made_t = raw * level * jnp.concatenate([out_cols[1]] * across, axis=1)
-    inputs_t[0, f_in : f_in + emb, :] = made_t.astype(BF16)
+    embedded_t = made_t.astype(BF16)
+    emb_t[0, 0:emb, 0:rows] = embedded_t
+
+    def emb_slot(p):
+        return emb_t.at[p // 2, pl.ds(0, emb), pl.ds(pl.multiple_of(p % 2 * rows, rows), rows)]
 
     @pl.loop(1, leaves)
     def _(i):
         p = leaf_order(i)
-        part = pl.ds(f_in, emb)
         pltpu.make_async_remote_copy(
-            src_ref=inputs_t.at[0, part], dst_ref=inputs_t.at[p, part], send_sem=emb_send,
+            src_ref=emb_slot(0), dst_ref=emb_slot(p), send_sem=emb_send.at[p],
             recv_sem=emb_recv.at[p], device_id=(g, flip(m, p, leaves)), device_id_type=MESH,
         ).start()
 
-    made = jnp.concatenate([made_t, jnp.zeros((128 - emb, rows), F32)], axis=0).T
-    embedding[...] = made[:, :emb].astype(BF16)
-
-    def one_group(p, tg, column):
-        margin = jnp.dot(selector[tg], inputs_t[p], preferred_element_type=F32)
-
-        def value(node, half):
+    embedding_t[...] = embedded_t
+
+    def one_group(pair, tg):
+        late = jnp.dot(selector[tg, :, f_in:], emb_t[pair], preferred_element_type=F32)
+
+        def value(node, part):
             at = place[node] * GROUP
             if 2 * node + 1 >= inner:
-                pair = node - inner // 2
-                low = leaf_mid[tg, pair * GROUP : (pair + 1) * GROUP, :]
-                gap = leaf_half[tg, pair * GROUP : (pair + 1) * GROUP, :]
+                leaf = node - inner // 2
+                low = leaf_mid[tg, leaf * GROUP : (leaf + 1) * GROUP, :]
+                gap = leaf_half[tg, leaf * GROUP : (leaf + 1) * GROUP, :]
             else:
-                left = value(2 * node + 1, half)
-                right = value(2 * node + 2, half)
+                left = value(2 * node + 1, part)
+                right = value(2 * node + 2, part)
                 low = left + right
                 gap = right - left
-            turn = jnp.tanh(margin[at : at + GROUP, half * 128 : (half + 1) * 128])
+            where = slice(part * 128, (part + 1) * 128)
+            turn = jnp.tanh(
+                margins[pair, tg, at : at + GROUP, where] + late[at : at + GROUP, where]
+            )
             return low + turn * gap
 
-        for half in range(rows // 128):
-            total = value(0, half)
-            where = slice(half * 128, (half + 1) * 128)
-            partial[column, :, where] += total[:8] + total[8:]
-
-    @pl.loop(0, leaves)
-    def _(i):
-        p = leaf_order(i)
-
-        @pl.when(i > 0)
+        for core in range(2):
+            for part in range(rows // 128):
+                total = value(0, core * (rows // 128) + part)
+                where = slice(part * 128, (part + 1) * 128)
+                partial[2 * pair + core, :, where] += total[:8] + total[8:]
+
+    def arrive(p):
+        pltpu.make_async_copy(emb_slot(p), emb_slot(p), emb_recv.at[p]).wait()
+
+    def leave(p):
+        pltpu.make_async_remote_copy(
+            src_ref=partial.at[p], dst_ref=partial_in.at[p], send_sem=score_send,
+            recv_sem=score_recv.at[p], device_id=(g, flip(m, p, leaves)), device_id_type=MESH,
+        ).start()
+
+    partial[...] = jnp.zeros(partial.shape, F32)
+    arrive(1)
+    early = groups // 2
+
+    @pl.loop(0, leaves // 2 * groups)
+    def _(step):
+        at = step + groups - early
+        turn = at // groups % (leaves // 2)
+        tg = at % groups
+        pair = leaf_order(2 * turn) // 2
+
+        @pl.when(jnp.logical_and(turn > 0, tg == 0))
         def _():
-            part = inputs_t.at[p, pl.ds(f_in, emb)]
-            pltpu.make_async_copy(part, part, emb_recv.at[p]).wait()
-
-        partial[p] = jnp.zeros(partial.shape[1:], F32)
-
-        @pl.loop(0, groups)
-        def _(tg):
-            one_group(p, tg, p)
-
-        @pl.when(i > 0)
+            arrive(2 * pair)
+            arrive(2 * pair + 1)
+
+        one_group(pair, tg)
+
+        @pl.when(jnp.logical_and(turn > 0, tg == groups - 1))
         def _():
-            pltpu.make_async_remote_copy(
-                src_ref=partial.at[p], dst_ref=partial_in.at[p], send_sem=score_send,
-                recv_sem=score_recv.at[p], device_id=(g, flip(m, p, leaves)), device_id_type=MESH,
-            ).start()
-
+            leave(2 * pair)
+            leave(2 * pair + 1)
+
+    leave(1)
     running = partial[0]
     for p in range(1, leaves):
         pltpu.make_async_copy(partial_in.at[p], partial_in.at[p], score_recv.at[p]).wait()
@@ -331,8 +370,8 @@
     pltpu.make_async_copy(feats.at[others], feats.at[others], feat_send).wait()
     block = outgoing.at[pl.ds(0, graphs - 1)]
     pltpu.make_async_copy(block, block, row_send).wait()
-    block = inputs_t.at[others, pl.ds(f_in, emb)]
-    pltpu.make_async_copy(block, block, emb_send).wait()
+    for p in range(1, leaves):
+        pltpu.make_async_copy(emb_slot(p), emb_slot(p), emb_send.at[p]).wait()
     pltpu.make_async_copy(partial.at[others], partial.at[others], score_send).wait()
 
 
@@ -362,10 +401,10 @@
     entries = neighbour_slot.shape[1]
     dma = pltpu.SemaphoreType.DMA
     vmem = pl.BlockSpec(memory_space=pltpu.VMEM)
-    embedding, scores = pl.pallas_call(
+    embedding_t, scores = pl.pallas_call(
         functools.partial(kernel, graphs, leaves),
         out_shape=(
-            jax.ShapeDtypeStruct((rows, emb), BF16),
+            jax.ShapeDtypeStruct((emb, rows), BF16),
             jax.ShapeDtypeStruct((1, rows), F32),
         ),
         in_specs=[vmem] * 13,
@@ -380,9 +419,10 @@
             pltpu.VMEM((groups, inner * GROUP, 512), BF16),
             pltpu.VMEM((groups, (inner + 1) // 2 * GROUP, 128), F32),
             pltpu.VMEM((groups, (inner + 1) // 2 * GROUP, 128), F32),
-            pltpu.VMEM((leaves, 512, rows), BF16),
+            pltpu.VMEM((f_in, 2 * rows), BF16),
+            pltpu.VMEM((leaves // 2, 128, 2 * rows), BF16),
+            pltpu.VMEM((leaves // 2, groups, inner * GROUP, 2 * rows), F32),
             pltpu.VMEM((rows, hid), F32),
-            pltpu.VMEM((emb, hid), BF16),
             pltpu.VMEM((2, emb, 128), F32),
             pltpu.VMEM((rows, 128), F32),
             pltpu.VMEM((rows, f_in), F32),
@@ -391,7 +431,7 @@
             dma,
             dma,
             dma,
-            dma,
+            dma((leaves,)),
             dma,
             dma((leaves,)),
             dma((leaves,)),
@@ -400,25 +440,25 @@
             dma((leaves,)),
         ],
         compiler_params=pltpu.CompilerParams(
-            collective_id=0, has_side_effects=True, vmem_limit_bytes=56 * 2**20
+            collective_id=0, has_side_effects=True, vmem_limit_bytes=62 * 2**20
         ),
         name="sage_forest",
     )(
         features,
-        send_rows.reshape(send_rows.shape[1:]),
-        neighbour_slot,
+        send_rows.reshape(send_rows.shape[1:]).T,
+        neighbour_slot.T,
         degree.reshape(1, rows),
         self_weight,
         neigh_weight,
         hidden_bias.reshape(1, hid),
-        out_weight,
+        out_weight.T,
         out_bias.reshape(1, emb),
         out_gain.reshape(1, emb),
         split_feature,
         threshold,
         leaf_value,
     )
-    return (embedding, scores.reshape(rows))
+    return (embedding_t.T, scores.reshape(rows))
 
 
 def solution(mesh):

time: 78.5 us -> 66.2 us (0.84)
  Pallas kernels: 71.7 us -> 63.4 us
  local copies, waits for them, and re-layouts: 5.81 us -> 1.94 us
    pallas_call x1, Pallas kernels: 71.7 us -> 63.4 us  [on_device(): pl.pallas_call(functools.partial(kernel, graphs, leaves), out_shape=(jax....]
    unnamed x11 -> x4, local copies, waits for them, and re-layouts: 5.81 us -> 1.94 us
where the time goes in v2:
time: 66.2 us; the launch traced here: 66 us
  Pallas kernels  63.4 us (96%)
  local copies, waits for them, and re-layouts  1.94 us (3%)
    pallas_call x1, Pallas kernels, on_device(): pl.pallas_call(functools.partial(kernel, graphs, leaves), out_shape=(jax....  63.4 us
    unnamed x4, local copies, waits for them, and re-layouts  1.94 us

profile of v2, /device:TPU:1, one launch (start us, length us, event | category | flops | bytes accessed | tf_op | source)
XLA Modules:
  0.0 66.0 jit_solution(17964715614981059049)
XLA Ops:
  0.6 63.4 %sage_forest.1 = (bf16[64,256]{1,0:T(8,128)(2,1)}, f32[1,256]{1,0:T(1,128)}) custom-call(bf16[256,384]{1,0:T(8,128)(2,1)} %features.1, s32[32,128]{1,0:T(8,128)} %bitcast.13, s32[16,256]{1,0:T(8,128)} %bitcast.14, s32[1,256]{1,0:T(1,128)} %bitcast.16, bf16[384,512]{1,0:T(8,128)(2,1)} %self_weight.1, bf16[384,512]{1,0:T(8,128)(2,1)} %neigh_weight.1, ...), custom_call_target="tpu_custom_call" | custom-call | tf_op jit(solution)/shard_map/sage_forest/pallas_call | solution.py:404
  64.1 0.0 copy-start
  64.1 1.4 %copy.17 = bf16[256,64]{0,1:T(8,128)(2,1)} copy(bf16[256,64]{0,1:T(8,128)(2,1)} %bitcast.12) | data formatting | bytes 65536
  65.5 0.0 copy-done
  65.5 0.6 copy.18
Async XLA Ops:
  64.1 1.4 %copy-start = (f32[1,256]{1,0:T(1,128)S(1)}, f32[1,256]{1,0:T(1,128)}, u32[]{:S(2)}) copy-start(f32[1,256]{1,0:T(1,128)} %get-tuple-element.5) | copy-start | bytes 3076

commit v3 on v2

--- a/solution.py
+++ b/solution.py
@@ -242,17 +242,22 @@
     gather_one(0)
     pl.semaphore_wait(barrier, graphs - 1 + leaves - 1)
 
-    @pl.loop(1, leaves)
-    def _(i):
-        p = leaf_order(i)
+    def send_ids(p):
         pltpu.make_async_remote_copy(
             src_ref=ids.at[0], dst_ref=ids.at[p], send_sem=ids_send, recv_sem=ids_recv.at[p],
             device_id=(g, flip(m, p, leaves)), device_id_type=MESH,
         ).start()
 
-    for p in (1,) + pair_order[1:]:
+    send_ids(1)
+    send_feats(0, 1)
+    send_part(0)
+
+    @pl.loop(2, leaves)
+    def _(i):
+        send_ids(leaf_order(i))
+
+    for p in pair_order[1:]:
         send_feats(0, p)
-    send_part(0)
     gather_one(1)
     send_part(1)
     build_selector()
@@ -336,29 +341,25 @@
         ).start()
 
     partial[...] = jnp.zeros(partial.shape, F32)
-    arrive(1)
-    early = groups // 2
-
-    @pl.loop(0, leaves // 2 * groups)
-    def _(step):
-        at = step + groups - early
-        turn = at // groups % (leaves // 2)
-        tg = at % groups
-        pair = leaf_order(2 * turn) // 2
-
-        @pl.when(jnp.logical_and(turn > 0, tg == 0))
+
+    @pl.loop(0, leaves // 2)
+    def _(i):
+        pair = leaf_order(2 * i) // 2
+
+        @pl.when(i > 0)
         def _():
             arrive(2 * pair)
-            arrive(2 * pair + 1)
-
-        one_group(pair, tg)
-
-        @pl.when(jnp.logical_and(turn > 0, tg == groups - 1))
+
+        arrive(2 * pair + 1)
+        for tg in range(groups):
+            one_group(pair, tg)
+
+        @pl.when(i > 0)
         def _():
             leave(2 * pair)
-            leave(2 * pair + 1)
-
-    leave(1)
+
+        leave(2 * pair + 1)
+
     running = partial[0]
     for p in range(1, leaves):
         pltpu.make_async_copy(partial_in.at[p], partial_in.at[p], score_recv.at[p]).wait()
@@ -404,8 +405,8 @@
     embedding_t, scores = pl.pallas_call(
         functools.partial(kernel, graphs, leaves),
         out_shape=(
-            jax.ShapeDtypeStruct((emb, rows), BF16),
-            jax.ShapeDtypeStruct((1, rows), F32),
+            pltpu.VMEM((emb, rows), BF16),
+            pltpu.VMEM((1, rows), F32),
         ),
         in_specs=[vmem] * 13,
         out_specs=(vmem, vmem),

time: 66.2 us -> 63.1 us (0.953)
  Pallas kernels: 63.4 us -> 61.1 us
  local copies, waits for them, and re-layouts: 1.94 us -> 1.18 us
    pallas_call x1, Pallas kernels: 63.4 us -> 61.1 us  [on_device(): pl.pallas_call(functools.partial(kernel, graphs, leaves), out_shape=(pltp...]
    unnamed x4 -> x2, local copies, waits for them, and re-layouts: 1.94 us -> 1.18 us
where the time goes in v3:
time: 63.1 us; the launch traced here: 62.9 us
  Pallas kernels  61.1 us (97%)
  local copies, waits for them, and re-layouts  1.18 us (2%)
  between operations  0.64 us (1%)
    pallas_call x1, Pallas kernels, on_device(): pl.pallas_call(functools.partial(kernel, graphs, leaves), out_shape=(pltp...  61.1 us

profile of v3, /device:TPU:1, one launch (start us, length us, event | category | flops | bytes accessed | tf_op | source)
XLA Modules:
  0.0 62.9 jit_solution(16706176497601175429)
XLA Ops:
  0.6 61.1 %sage_forest.1 = (bf16[64,256]{1,0:T(8,128)(2,1)S(1)}, f32[1,256]{1,0:T(1,128)S(1)}) custom-call(bf16[256,384]{1,0:T(8,128)(2,1)} %features.1, s32[32,128]{1,0:T(8,128)} %bitcast.14, s32[16,256]{1,0:T(8,128)} %bitcast.15, s32[1,256]{1,0:T(1,128)} %bitcast.17, bf16[384,512]{1,0:T(8,128)(2,1)} %self_weight.1, bf16[384,512]{1,0:T(8,128)(2,1)} %neigh_weight.1, ...), custom_call_target="tpu_custom_call" | custom-call | tf_op jit(solution)/shard_map/sage_forest/pallas_call | solution.py:405
  61.7 0.6 copy.17
  62.4 0.6 copy.18

commit v4 on v3

--- a/solution.py
+++ b/solution.py
@@ -10,6 +10,8 @@
 NORM_EPS = 1e-05
 CAP = 32
 GROUP = 16
+SIDE = 4
+EARLY = 256
 BF16 = jnp.bfloat16
 F32 = jnp.float32
 MESH = pl.DeviceIdType.MESH
@@ -61,6 +63,7 @@
     feats,
     ids,
     outgoing,
+    far,
     arrived,
     slot_ids,
     counts,
@@ -79,6 +82,7 @@
     feat_send,
     ids_send,
     row_send,
+    far_send,
     emb_send,
     score_send,
     feat_recv,
@@ -96,21 +100,33 @@
     width = leaves * CAP
     groups = trees // GROUP
     place = post_order(inner)
+    late_at = f_in - EARLY
     lanes = lax.broadcasted_iota(jnp.int32, (1, 128), 1)
 
     barrier = pltpu.get_barrier_semaphore()
 
-    @pl.loop(1, graphs)
-    def _(step):
-        pl.semaphore_signal(
-            barrier, inc=1, device_id=(lax.rem(g + step, graphs), m), device_id_type=MESH
-        )
-
-    @pl.loop(1, leaves)
-    def _(step):
-        pl.semaphore_signal(
-            barrier, inc=1, device_id=(g, flip(m, step, leaves)), device_id_type=MESH
-        )
+    x, z = g // SIDE, g % SIDE
+
+    def spot(dx, dz):
+        return (x + dx) % SIDE * SIDE + (z + dz) % SIDE
+
+    def near(i):
+        return i + i // 2
+
+    def greet(graph, leaf):
+        pl.semaphore_signal(barrier, inc=1, device_id=(graph, leaf), device_id_type=MESH)
+
+    @pl.loop(1, SIDE * leaves)
+    def _(i):
+        greet(spot(0, i // leaves), flip(m, i % leaves, leaves))
+
+    @pl.loop(0, 2 * leaves)
+    def _(i):
+        greet(spot(1 + 2 * (i // leaves), 0), flip(m, i % leaves, leaves))
+
+    for dx, dz in ((2, 0), (1, 1), (1, 3), (3, 1), (3, 3)):
+        greet(spot(dx, dz), m)
+    greeted = SIDE * leaves - 1 + 2 * leaves + 5
 
     devices = graphs * leaves
     ids[0] = send_rows[...]
@@ -140,20 +156,22 @@
             if p % 2 == 0:
                 send_feats(p, 1)
         mine = pltpu.roll(ids[p], devices - m, axis=1)
-        pieces = []
-        for target in range(graphs):
-            column = mine[:, target * leaves : target * leaves + 1]
-            pieces.append((column == row_lanes).astype(F32).astype(BF16))
-        picked = jnp.dot(
-            jnp.concatenate(pieces, axis=0), feats[p], preferred_element_type=F32
-        ).astype(BF16)
+        picked = pick(mine, range(0, devices, leaves), p)
         for target in range(graphs):
             outgoing[target, pl.ds(p * CAP, CAP), :] = picked[target * CAP : (target + 1) * CAP]
 
+    def pick(mine, columns, slot):
+        pieces = []
+        for column in columns:
+            pieces.append((mine[:, column : column + 1] == row_lanes).astype(F32).astype(BF16))
+        return jnp.dot(
+            jnp.concatenate(pieces, axis=0), feats[slot], preferred_element_type=F32
+        ).astype(BF16)
+
     def send_part(p):
-        @pl.loop(1, graphs)
-        def _(step):
-            target = lax.rem(g + step, graphs)
+        @pl.loop(1, 9)
+        def _(i):
+            target = spot(near(i // 3), near(i % 3))
             part = pl.ds(p * CAP, CAP)
             pltpu.make_async_remote_copy(
                 src_ref=outgoing.at[target, part],
@@ -162,6 +180,58 @@
                 recv_sem=row_recv.at[g],
                 device_id=(target, m),
                 device_id_type=MESH,
+            ).start()
+
+    opposite = (spot(2, 0), spot(0, 2))
+
+    def send_far_feats(axis):
+        slot = leaves + axis
+        for ref, send_sem, recv_sem in ((ids, ids_send, ids_recv), (feats, feat_send, feat_recv)):
+            pltpu.make_async_remote_copy(
+                src_ref=ref.at[0], dst_ref=ref.at[slot], send_sem=send_sem,
+                recv_sem=recv_sem.at[slot], device_id=(opposite[axis], m), device_id_type=MESH,
+            ).start()
+
+    def gather_far(axis):
+        slot = leaves + axis
+        pltpu.make_async_copy(ids.at[slot], ids.at[slot], ids_recv.at[slot]).wait()
+        pltpu.make_async_copy(feats.at[slot], feats.at[slot], feat_recv.at[slot]).wait()
+        if axis == 0:
+            mine = pltpu.roll(ids[slot], devices - x * (SIDE * leaves), axis=1)
+            stride = leaves
+        else:
+            mine = pltpu.roll(ids[slot], devices - z * leaves, axis=1)
+            stride = SIDE * leaves
+        for half in range(2):
+            columns = []
+            for other in range(2 * half, 2 * half + 2):
+                columns.extend(range(other * stride, other * stride + leaves))
+            picked = pick(mine, columns, slot)
+            for i in range(2 * leaves):
+                far[axis, 2 * leaves * half + i] = picked[i * CAP : (i + 1) * CAP]
+
+    def send_far(axis):
+        source = opposite[axis]
+
+        def piece(i):
+            turn, p = i // leaves, i % leaves
+            if axis == 0:
+                graph, other = spot(0, turn), (z + turn) % SIDE
+            else:
+                graph, other = spot(near(turn), 0), (x + near(turn)) % SIDE
+            leaf = flip(m, p, leaves)
+            part = pl.ds(p * CAP, CAP)
+            return far.at[axis, other * leaves + leaf], arrived.at[source, part], graph, leaf
+
+        here, there, _, _ = piece(0)
+        pltpu.make_async_copy(here, there, row_recv.at[source]).start()
+
+        @pl.loop(1, (SIDE - axis) * leaves)
+        def _(i):
+            src, dst, graph, leaf = piece(i)
+            pltpu.make_async_remote_copy(
+                src_ref=src, dst_ref=dst, send_sem=far_send.at[axis],
+                recv_sem=row_recv.at[source], device_id=(graph, leaf), device_id_type=MESH,
             ).start()
 
     def build_selector():
@@ -194,7 +264,7 @@
                 leaf_mid[tg, where, :] = jnp.broadcast_to((left + right) * scale, (GROUP, 128))
                 leaf_half[tg, where, :] = jnp.broadcast_to((right - left) * scale, (GROUP, 128))
 
-    def build_counts():
+    def start_counts():
         degrees = jnp.broadcast_to(degree[...].astype(F32), (128, rows)).T
         degree_col[...] = degrees
         named_all = jnp.concatenate(
@@ -202,19 +272,22 @@
         ).T ^ (m * CAP)
         for j in range(entries):
             named = jnp.broadcast_to(named_all[:, j : j + 1], (rows, 128))
-            slot_ids[j] = jnp.where(degrees > j + 0.5, named, -1)
-
-        @pl.loop(0, graphs)
+            slot_ids[j] = jnp.where(degrees > j + 0.5, named, -1).astype(jnp.int16)
+
+    def build_counts(first, last):
+        one, none = jnp.ones((128, 128), BF16), jnp.zeros((128, 128), BF16)
+
+        @pl.loop(first, last)
         def _(source):
             for half in range(width // 128):
-                here = lanes + (source * width + half * 128)
+                here = jnp.broadcast_to(lanes + (source * width + half * 128), (128, 128)).astype(
+                    jnp.int16
+                )
                 for part in range(0, rows, 128):
-                    total = jnp.zeros((128, 128), F32)
+                    total = none
                     for j in range(entries):
-                        total = total + jnp.where(slot_ids[j, part : part + 128] == here, 1.0, 0.0)
-                    counts[source, part : part + 128, half * 128 : (half + 1) * 128] = total.astype(
-                        BF16
-                    )
+                        total = total + jnp.where(slot_ids[j, part : part + 128] == here, one, none)
+                    counts[source, part : part + 128, half * 128 : (half + 1) * 128] = total
 
     def build_rest():
         own_term[...] = (
@@ -224,23 +297,25 @@
             wide_row = jnp.concatenate([row[...], jnp.zeros((1, 128 - emb), F32)], axis=1)
             out_cols[place_at] = jnp.broadcast_to(wide_row, (128, 128)).T[:emb]
         for pair in range(leaves // 2):
-            emb_t[pair, emb:, :] = jnp.ones((128 - emb, 2 * rows), BF16)
+            emb_t[pair, late_at + emb :, :] = jnp.ones((128 - emb, 2 * rows), BF16)
 
     def build_margins():
         @pl.loop(0, leaves // 2)
         def _(pair):
             for core in range(2):
-                feat_t[:, core * rows : (core + 1) * rows] = feats[2 * pair + core].T
-
-            @pl.loop(0, groups)
-            def _(tg):
+                turned = feats[2 * pair + core].T
+                where = slice(core * rows, (core + 1) * rows)
+                feat_t[:, where] = turned[:EARLY]
+                emb_t[pair, 0 : f_in - EARLY, where] = turned[EARLY:]
+
+            for tg in range(groups):
                 margins[pair, tg] = jnp.dot(
-                    selector[tg, :, :f_in], feat_t[...], preferred_element_type=F32
+                    selector[tg, :, :EARLY], feat_t[...], preferred_element_type=F32
                 )
 
     pair_order = (0, 2, 6, 4) if leaves == 8 else tuple(range(0, leaves, 2))
     gather_one(0)
-    pl.semaphore_wait(barrier, graphs - 1 + leaves - 1)
+    pl.semaphore_wait(barrier, greeted)
 
     def send_ids(p):
         pltpu.make_async_remote_copy(
@@ -250,6 +325,8 @@
 
     send_ids(1)
     send_feats(0, 1)
+    for axis in range(2):
+        send_far_feats(axis)
     send_part(0)
 
     @pl.loop(2, leaves)
@@ -261,22 +338,33 @@
     gather_one(1)
     send_part(1)
     build_selector()
-    for at, first in enumerate(pair_order[1:]):
+    for axis in range(2):
+        gather_far(axis)
+        send_far(axis)
+    start_counts()
+    for turn, first in enumerate(pair_order[1:]):
         for p in (first, first + 1):
             gather_one(p)
             send_part(p)
-        if at == 0:
-            build_rest()
-    build_counts()
+        build_counts(turn * 5, turn * 5 + 5)
+    build_counts(15, graphs)
+    build_rest()
     build_margins()
 
     summed[...] = jnp.dot(counts[g], outgoing[g], preferred_element_type=F32)
 
-    @pl.loop(1, graphs)
-    def _(step):
-        source = lax.rem(g + graphs - step, graphs)
+    def add(source):
         pltpu.make_async_copy(arrived.at[source], arrived.at[source], row_recv.at[source]).wait()
         summed[...] += jnp.dot(counts[source], arrived[source], preferred_element_type=F32)
+
+    @pl.loop(0, 2 * SIDE - 1)
+    def _(i):
+        low = i // SIDE
+        add(spot(2 + low * (near(i % SIDE) - 2), i % SIDE + low * (2 - i % SIDE)))
+
+    @pl.loop(1, 9)
+    def _(i):
+        add(spot(near(i // 3), near(i % 3)))
 
     by = jnp.concatenate([degree_col[...]] * (f_in // 128), axis=1)
     mean = (summed[...] / by).astype(BF16)
@@ -290,10 +378,10 @@
     level = lax.rsqrt(jnp.sum(raw * raw, axis=0, keepdims=True) * (1.0 / emb) + NORM_EPS)
     made_t = raw * level * jnp.concatenate([out_cols[1]] * across, axis=1)
     embedded_t = made_t.astype(BF16)
-    emb_t[0, 0:emb, 0:rows] = embedded_t
+    emb_t[0, late_at : late_at + emb, 0:rows] = embedded_t
 
     def emb_slot(p):
-        return emb_t.at[p // 2, pl.ds(0, emb), pl.ds(pl.multiple_of(p % 2 * rows, rows), rows)]
+        return emb_t.at[p // 2, pl.ds(late_at, emb), pl.ds(pl.multiple_of(p % 2 * rows, rows), rows)]
 
     @pl.loop(1, leaves)
     def _(i):
@@ -306,7 +394,7 @@
     embedding_t[...] = embedded_t
 
     def one_group(pair, tg):
-        late = jnp.dot(selector[tg, :, f_in:], emb_t[pair], preferred_element_type=F32)
+        late = jnp.dot(selector[tg, :, EARLY:], emb_t[pair], preferred_element_type=F32)
 
         def value(node, part):
             at = place[node] * GROUP
@@ -366,14 +454,18 @@
         running = running + partial_in[p]
     scores[...] = jnp.sum(running, axis=0, keepdims=True)
 
-    others = pl.ds(0, leaves - 1)
+    others = pl.ds(0, leaves + 1)
     pltpu.make_async_copy(ids.at[others], ids.at[others], ids_send).wait()
     pltpu.make_async_copy(feats.at[others], feats.at[others], feat_send).wait()
-    block = outgoing.at[pl.ds(0, graphs - 1)]
+    for axis in range(2):
+        block = far.at[axis, pl.ds(0, (SIDE - axis) * leaves - 1)]
+        pltpu.make_async_copy(block, block, far_send.at[axis]).wait()
+    block = outgoing.at[pl.ds(0, 8)]
     pltpu.make_async_copy(block, block, row_send).wait()
     for p in range(1, leaves):
         pltpu.make_async_copy(emb_slot(p), emb_slot(p), emb_send.at[p]).wait()
-    pltpu.make_async_copy(partial.at[others], partial.at[others], score_send).wait()
+    block = partial.at[pl.ds(0, leaves - 1)]
+    pltpu.make_async_copy(block, block, score_send).wait()
 
 
 def on_device(
@@ -411,17 +503,18 @@
         in_specs=[vmem] * 13,
         out_specs=(vmem, vmem),
         scratch_shapes=[
-            pltpu.VMEM((leaves, rows, f_in), BF16),
-            pltpu.VMEM((leaves, CAP, graphs * leaves), jnp.int32),
+            pltpu.VMEM((leaves + 2, rows, f_in), BF16),
+            pltpu.VMEM((leaves + 2, CAP, graphs * leaves), jnp.int32),
             pltpu.VMEM((graphs, width, f_in), BF16),
+            pltpu.VMEM((2, SIDE * leaves, CAP, f_in), BF16),
             pltpu.VMEM((graphs, width, f_in), BF16),
-            pltpu.VMEM((entries, rows, 128), jnp.int32),
+            pltpu.VMEM((entries, rows, 128), jnp.int16),
             pltpu.VMEM((graphs, rows, width), BF16),
             pltpu.VMEM((groups, inner * GROUP, 512), BF16),
             pltpu.VMEM((groups, (inner + 1) // 2 * GROUP, 128), F32),
             pltpu.VMEM((groups, (inner + 1) // 2 * GROUP, 128), F32),
-            pltpu.VMEM((f_in, 2 * rows), BF16),
-            pltpu.VMEM((leaves // 2, 128, 2 * rows), BF16),
+            pltpu.VMEM((EARLY, 2 * rows), BF16),
+            pltpu.VMEM((leaves // 2, 512 - EARLY, 2 * rows), BF16),
             pltpu.VMEM((leaves // 2, groups, inner * GROUP, 2 * rows), F32),
             pltpu.VMEM((rows, hid), F32),
             pltpu.VMEM((2, emb, 128), F32),
@@ -432,10 +525,11 @@
             dma,
             dma,
             dma,
+            dma((2,)),
             dma((leaves,)),
             dma,
-            dma((leaves,)),
-            dma((leaves,)),
+            dma((leaves + 2,)),
+            dma((leaves + 2,)),
             dma((graphs,)),
             dma((leaves,)),
             dma((leaves,)),

time: 63.1 us -> 60.8 us (0.964)
  Pallas kernels: 61.1 us -> 58.8 us
    pallas_call x1, Pallas kernels: 61.1 us -> 58.8 us  [on_device(): pl.pallas_call(functools.partial(kernel, graphs, leaves), out_shape=(pltp...]
where the time goes in v4:
time: 60.8 us; the launch traced here: 60.6 us
  Pallas kernels  58.8 us (97%)
  local copies, waits for them, and re-layouts  1.18 us (2%)
  between operations  0.64 us (1%)
    pallas_call x1, Pallas kernels, on_device(): pl.pallas_call(functools.partial(kernel, graphs, leaves), out_shape=(pltp...  58.8 us

profile of v4, /device:TPU:1, one launch (start us, length us, event | category | flops | bytes accessed | tf_op | source)
XLA Modules:
  0.0 60.6 jit_solution(7511497411033726431)
XLA Ops:
  0.6 58.8 %sage_forest.1 = (bf16[64,256]{1,0:T(8,128)(2,1)S(1)}, f32[1,256]{1,0:T(1,128)S(1)}) custom-call(bf16[256,384]{1,0:T(8,128)(2,1)} %features.1, s32[32,128]{1,0:T(8,128)} %bitcast.14, s32[16,256]{1,0:T(8,128)} %bitcast.15, s32[1,256]{1,0:T(1,128)} %bitcast.17, bf16[384,512]{1,0:T(8,128)(2,1)} %self_weight.1, bf16[384,512]{1,0:T(8,128)(2,1)} %neigh_weight.1, ...), custom_call_target="tpu_custom_call" | custom-call | tf_op jit(solution)/shard_map/sage_forest/pallas_call | solution.py:497
  59.5 0.6 %copy.17 = bf16[256,64]{0,1:T(8,128)(2,1)} copy(bf16[256,64]{0,1:T(8,128)(2,1)S(1)} %bitcast.11) | data formatting | bytes 65536
  60.1 0.6 copy.18

commit v5 on v4

--- a/solution.py
+++ b/solution.py
@@ -353,18 +353,23 @@
 
     summed[...] = jnp.dot(counts[g], outgoing[g], preferred_element_type=F32)
 
-    def add(source):
-        pltpu.make_async_copy(arrived.at[source], arrived.at[source], row_recv.at[source]).wait()
-        summed[...] += jnp.dot(counts[source], arrived[source], preferred_element_type=F32)
-
-    @pl.loop(0, 2 * SIDE - 1)
-    def _(i):
-        low = i // SIDE
-        add(spot(2 + low * (near(i % SIDE) - 2), i % SIDE + low * (2 - i % SIDE)))
-
-    @pl.loop(1, 9)
-    def _(i):
-        add(spot(near(i // 3), near(i % 3)))
+    def add_all(total, sources):
+        for source in sources:
+            pltpu.make_async_copy(
+                arrived.at[source], arrived.at[source], row_recv.at[source]
+            ).wait()
+        for source in sources:
+            total = total + jnp.dot(
+                counts[source], arrived[source], preferred_element_type=F32
+            )
+        return total
+
+    steps = (0, 1, 3)
+    summed[...] = add_all(
+        summed[...], [spot(2, dz) for dz in range(SIDE)] + [spot(dx, 2) for dx in steps]
+    )
+    hops = [spot(dx, dz) for dx in steps for dz in steps][1:]
+    summed[...] = add_all(summed[...], hops)
 
     by = jnp.concatenate([degree_col[...]] * (f_in // 128), axis=1)
     mean = (summed[...] / by).astype(BF16)

time: 60.8 us -> 58.3 us (0.959)
  Pallas kernels: 58.8 us -> 56.3 us
    pallas_call x1, Pallas kernels: 58.8 us -> 56.3 us  [on_device(): pl.pallas_call(functools.partial(kernel, graphs, leaves), out_shape=(pltp...]
where the time goes in v5:
time: 58.3 us; the launch traced here: 58.2 us
  Pallas kernels  56.3 us (97%)
  local copies, waits for them, and re-layouts  1.18 us (2%)
  between operations  0.64 us (1%)
    pallas_call x1, Pallas kernels, on_device(): pl.pallas_call(functools.partial(kernel, graphs, leaves), out_shape=(pltp...  56.3 us
    unnamed x2, local copies, waits for them, and re-layouts  1.18 us

profile of v5, /device:TPU:1, one launch (start us, length us, event | category | flops | bytes accessed | tf_op | source)
XLA Modules:
  0.0 58.2 jit_solution(15385757354163398391)
XLA Ops:
  0.6 56.3 %sage_forest.1 = (bf16[64,256]{1,0:T(8,128)(2,1)S(1)}, f32[1,256]{1,0:T(1,128)S(1)}) custom-call(bf16[256,384]{1,0:T(8,128)(2,1)} %features.1, s32[32,128]{1,0:T(8,128)} %bitcast.14, s32[16,256]{1,0:T(8,128)} %bitcast.15, s32[1,256]{1,0:T(1,128)} %bitcast.17, bf16[384,512]{1,0:T(8,128)(2,1)} %self_weight.1, bf16[384,512]{1,0:T(8,128)(2,1)} %neigh_weight.1, ...), custom_call_target="tpu_custom_call" | custom-call | tf_op jit(solution)/shard_map/sage_forest/pallas_call | solution.py:502
  57.0 0.6 %copy.17 = bf16[256,64]{0,1:T(8,128)(2,1)} copy(bf16[256,64]{0,1:T(8,128)(2,1)S(1)} %bitcast.11) | data formatting | bytes 65536
  57.6 0.6 copy.18

commit v6 on v5

--- a/solution.py
+++ b/solution.py
@@ -116,12 +116,10 @@
     def greet(graph, leaf):
         pl.semaphore_signal(barrier, inc=1, device_id=(graph, leaf), device_id_type=MESH)
 
-    @pl.loop(1, SIDE * leaves)
-    def _(i):
+    for i in range(1, SIDE * leaves):
         greet(spot(0, i // leaves), flip(m, i % leaves, leaves))
 
-    @pl.loop(0, 2 * leaves)
-    def _(i):
+    for i in range(2 * leaves):
         greet(spot(1 + 2 * (i // leaves), 0), flip(m, i % leaves, leaves))
 
     for dx, dz in ((2, 0), (1, 1), (1, 3), (3, 1), (3, 3)):
@@ -169,8 +167,7 @@
         ).astype(BF16)
 
     def send_part(p):
-        @pl.loop(1, 9)
-        def _(i):
+        for i in range(1, 9):
             target = spot(near(i // 3), near(i % 3))
             part = pl.ds(p * CAP, CAP)
             pltpu.make_async_remote_copy(
@@ -226,8 +223,7 @@
         here, there, _, _ = piece(0)
         pltpu.make_async_copy(here, there, row_recv.at[source]).start()
 
-        @pl.loop(1, (SIDE - axis) * leaves)
-        def _(i):
+        for i in range(1, (SIDE - axis) * leaves):
             src, dst, graph, leaf = piece(i)
             pltpu.make_async_remote_copy(
                 src_ref=src, dst_ref=dst, send_sem=far_send.at[axis],
@@ -329,8 +325,7 @@
         send_far_feats(axis)
     send_part(0)
 
-    @pl.loop(2, leaves)
-    def _(i):
+    for i in range(2, leaves):
         send_ids(leaf_order(i))
 
     for p in pair_order[1:]:
@@ -386,10 +381,9 @@
     emb_t[0, late_at : late_at + emb, 0:rows] = embedded_t
 
     def emb_slot(p):
-        return emb_t.at[p // 2, pl.ds(late_at, emb), pl.ds(pl.multiple_of(p % 2 * rows, rows), rows)]
-
-    @pl.loop(1, leaves)
-    def _(i):
+        return emb_t.at[p // 2, pl.ds(late_at, emb), pl.ds(p % 2 * rows if isinstance(p, int) else pl.multiple_of(p % 2 * rows, rows), rows)]
+
+    for i in range(1, leaves):
         p = leaf_order(i)
         pltpu.make_async_remote_copy(
             src_ref=emb_slot(0), dst_ref=emb_slot(p), send_sem=emb_send.at[p],

time: 58.3 us -> 55.9 us (0.959)
  Pallas kernels: 56.3 us -> 53.9 us
    pallas_call x1, Pallas kernels: 56.3 us -> 53.9 us  [on_device(): pl.pallas_call(functools.partial(kernel, graphs, leaves), out_shape=(pltp...]
where the time goes in v6:
time: 55.9 us; the launch traced here: 55.8 us
  Pallas kernels  53.9 us (96%)
  local copies, waits for them, and re-layouts  1.18 us (2%)
  between operations  0.64 us (1%)
    pallas_call x1, Pallas kernels, on_device(): pl.pallas_call(functools.partial(kernel, graphs, leaves), out_shape=(pltp...  53.9 us
    unnamed x2, local copies, waits for them, and re-layouts  1.18 us

profile of v6, /device:TPU:1, one launch (start us, length us, event | category | flops | bytes accessed | tf_op | source)
XLA Modules:
  0.0 55.8 jit_solution(7937988574631821181)
XLA Ops:
  0.6 53.9 %sage_forest.1 = (bf16[64,256]{1,0:T(8,128)(2,1)S(1)}, f32[1,256]{1,0:T(1,128)S(1)}) custom-call(bf16[256,384]{1,0:T(8,128)(2,1)} %features.1, s32[32,128]{1,0:T(8,128)} %bitcast.14, s32[16,256]{1,0:T(8,128)} %bitcast.15, s32[1,256]{1,0:T(1,128)} %bitcast.17, bf16[384,512]{1,0:T(8,128)(2,1)} %self_weight.1, bf16[384,512]{1,0:T(8,128)(2,1)} %neigh_weight.1, ...), custom_call_target="tpu_custom_call" | custom-call | tf_op jit(solution)/shard_map/sage_forest/pallas_call | solution.py:496
  54.6 0.6 %copy.17 = bf16[256,64]{0,1:T(8,128)(2,1)} copy(bf16[256,64]{0,1:T(8,128)(2,1)S(1)} %bitcast.11) | data formatting | bytes 65536
  55.2 0.6 %copy.18 = f32[256]{0:T(256)} copy(f32[256]{0:T(256)S(1)} %bitcast.12) | data formatting | bytes 2048

commit v7 on v6

--- a/solution.py
+++ b/solution.py
@@ -333,14 +333,16 @@
     gather_one(1)
     send_part(1)
     build_selector()
-    for axis in range(2):
-        gather_far(axis)
-        send_far(axis)
+    gather_far(0)
+    send_far(0)
     start_counts()
     for turn, first in enumerate(pair_order[1:]):
         for p in (first, first + 1):
             gather_one(p)
             send_part(p)
+        if turn == 0:
+            gather_far(1)
+            send_far(1)
         build_counts(turn * 5, turn * 5 + 5)
     build_counts(15, graphs)
     build_rest()

time: 55.9 us -> 54.4 us (0.973)
  Pallas kernels: 53.9 us -> 52.4 us
    pallas_call x1, Pallas kernels: 53.9 us -> 52.4 us  [on_device(): pl.pallas_call(functools.partial(kernel, graphs, leaves), out_shape=(pltp...]
where the time goes in v7:
time: 54.4 us; the launch traced here: 54.2 us
  Pallas kernels  52.4 us (96%)
  local copies, waits for them, and re-layouts  1.18 us (2%)
  between operations  0.64 us (1%)
    pallas_call x1, Pallas kernels, on_device(): pl.pallas_call(functools.partial(kernel, graphs, leaves), out_shape=(pltp...  52.4 us
    unnamed x2, local copies, waits for them, and re-layouts  1.18 us

profile of v7, /device:TPU:1, one launch (start us, length us, event | category | flops | bytes accessed | tf_op | source)
XLA Modules:
  0.0 54.2 jit_solution(6166202325853140010)
XLA Ops:
  0.6 52.4 %sage_forest.1 = (bf16[64,256]{1,0:T(8,128)(2,1)S(1)}, f32[1,256]{1,0:T(1,128)S(1)}) custom-call(bf16[256,384]{1,0:T(8,128)(2,1)} %features.1, s32[32,128]{1,0:T(8,128)} %bitcast.14, s32[16,256]{1,0:T(8,128)} %bitcast.15, s32[1,256]{1,0:T(1,128)} %bitcast.17, bf16[384,512]{1,0:T(8,128)(2,1)} %self_weight.1, bf16[384,512]{1,0:T(8,128)(2,1)} %neigh_weight.1, ...), custom_call_target="tpu_custom_call" | custom-call | tf_op jit(solution)/shard_map/sage_forest/pallas_call | solution.py:498
  53.0 0.6 %copy.17 = bf16[256,64]{0,1:T(8,128)(2,1)} copy(bf16[256,64]{0,1:T(8,128)(2,1)S(1)} %bitcast.11) | data formatting | bytes 65536
  53.7 0.6 %copy.18 = f32[256]{0:T(256)} copy(f32[256]{0:T(256)S(1)} %bitcast.12) | data formatting | bytes 2048
